TPU v7x, 512 devices: a whole 4x8x8 slice. The times are simulated.
512 devices in a mesh: hid: 32 (over y, z_lo), col: 16 (over x, z_hi, core).
Axes of the slice: x: 4, y: 8, z: 8 (z_hi: 2, z_lo: 4; z = z_hi * 4 + z_lo), core: 2. Of those that a mesh axis runs over, the one named last changes fastest.
Arguments:
- inputs: bfloat16 [15360, 28672], P('col', 'hid'), may hold values from -6 to 6
- out_grads: bfloat16 [15360, 8192], P('col', 'hid'), may hold values from -6 to 6
- proj_in: bfloat16 [96, 28672], P(None, 'hid'), may hold values from -0.03125 to 0.03125
- proj_out: bfloat16 [192, 8192], P(None, 'hid'), may hold values from -0.0625 to 0.0625
- curvature: bfloat16 [18432, 18432], P('hid', 'col'), may hold values from -0.119628906 to 0.119628906
Outputs:
- applied: float32 [480, 18432], P('hid', 'col')
- curvature_new: bfloat16 [18432, 18432], P('hid', 'col')
All inputs are finite; a program needn't handle non-finite values.
Results may differ from a plain program's by a relative error of at most 0.012.
Values may be sent and summed in bfloat16 or wider, within the bound.
A program may use at most 64 MiB of HBM per device.

v0:
```python
import jax
import jax.numpy as jnp
from jax import lax
from jax.sharding import PartitionSpec as P

PIN = 96
POUT = 192
SEQ = 32


gram_weight = 1.0 / 64.0
apply_weight = 1.0 / 16.0


def joined_along(pieces, dim):
    pieces = jnp.moveaxis(pieces, 0, dim)
    dims = pieces.shape
    return pieces.reshape(*dims[:dim], dims[dim] * dims[dim + 1], *dims[dim + 2 :])


def sent_to_all(value, axis):
    count = lax.axis_size(axis)
    return lax.all_to_all(
        jnp.broadcast_to(value[None], (count, *value.shape)), axis, 0, 0, tiled=True
    )


def collect(value, axis, dim):
    return joined_along(sent_to_all(value, axis), dim)


def cut_along(value, dim, count):
    before, after = (value.shape[:dim], value.shape[dim + 1 :])
    return jnp.moveaxis(value.reshape(*before, count, -1, *after), dim, 0)


def sum_at_owner(value, axis, dim):
    pieces = cut_along(value, dim, lax.axis_size(axis))
    arrived = lax.all_to_all(pieces, axis, split_axis=0, concat_axis=0, tiled=True)
    return arrived.astype(jnp.float32).sum(axis=0)


def pair_rows(feat, grad, width):
    count = feat.shape[0] // SEQ
    part = feat.reshape(count, SEQ, PIN)
    formed = jnp.einsum(
        "eti,etj->eij", part, grad.reshape(count, SEQ, POUT), preferred_element_type=jnp.float32
    )
    return formed.reshape(count, width * POUT).astype(jnp.bfloat16)


def per_device(inputs, out_grads, proj_in, proj_out, curvature):
    contract = (((1,), (1,)), ((), ()))
    feat_part = lax.dot_general(inputs, proj_in, contract, preferred_element_type=jnp.float32)
    grad_part = lax.dot_general(out_grads, proj_out, contract, preferred_element_type=jnp.float32)
    hid_count = lax.axis_size("hid")
    col_count = lax.axis_size("col")
    hid_place = lax.axis_index("hid")
    k_width = PIN // hid_count
    n_width = PIN // col_count
    feat, grad = lax.psum((feat_part, grad_part), "hid")
    feat = feat.astype(jnp.bfloat16)
    grad = grad.astype(jnp.bfloat16)
    own_rows = pair_rows(feat, grad, PIN)
    own_count = own_rows.shape[0]
    own_block = lax.dynamic_slice_in_dim(own_rows, hid_place * (k_width * POUT), k_width * POUT, 1)
    rows_k = collect(own_block, "col", 0)
    spread_rows = lax.all_to_all(
        own_rows.reshape(own_count, col_count, n_width * POUT),
        "col",
        split_axis=1,
        concat_axis=0,
        tiled=True,
    )
    rows_n = spread_rows.reshape(own_count * col_count, n_width * POUT)
    examples = rows_k.shape[0]
    gram = lax.dot_general(
        rows_k, rows_n, (((0,), (0,)), ((), ())), preferred_element_type=jnp.float32
    )
    curvature_new = (curvature.astype(jnp.float32) + gram * (gram_weight / examples)).astype(
        jnp.bfloat16
    )
    applied = sum_at_owner(
        (jnp.dot(rows_k, curvature_new, preferred_element_type=jnp.float32) * apply_weight).astype(
            jnp.bfloat16
        ),
        "hid",
        0,
    )
    return (applied, curvature_new)


def solution(mesh):
    in_specs = (P("col", "hid"), P("col", "hid"), P(None, "hid"), P(None, "hid"), P("hid", "col"))
    out_specs = (P("hid", "col"), P("hid", "col"))
    return jax.shard_map(
        per_device, mesh=mesh, in_specs=in_specs, out_specs=out_specs, check_vma=False
    )
```

profile of v0, /device:TPU:6, one launch (start us, length us, event | category | flops | bytes accessed | tf_op | source)
XLA Modules:
  0.0 290.9 jit_solution(2550040175233812339)
XLA Ops:
  0.6 0.0 copy-start
  0.6 0.0 copy-start.1
  0.7 1.5 fusion.4
  2.2 0.1 copy-done
  2.3 0.0 copy-done.1
  2.3 0.7 fusion.3
  3.0 170.0 %all-reduce.2 = (bf16[960,96]{0,1:T(8,128)(2,1)}, bf16[960,192]{0,1:T(8,128)(2,1)S(1)}) all-reduce(f32[960,96]{0,1:T(8,128)S(1)} %fusion.3, f32[960,192]{0,1:T(8,128)S(1)} %fusion.4), channel_id=1, replica_groups=mesh['hid'=32,'col'=16] {'hid'}, use_global_device_ids=true, to_apply=%region_0.0 | all-reduce | flops 276480 | bytes 1658880 | tf_op jit(solution)/shard_map/psum | solution.py:61
  172.9 1.0 copy.10
  173.9 1.1 copy.9
  175.0 1.6 convolution_convert_fusion
  176.7 2.7 convert_element_type.31
  179.4 0.9 constant_dynamic-slice_fusion
  180.3 0.9 broadcast_in_dim.2
  181.2 10.5 %all-to-all-start = ((bf16[16,30,576]{2,1,0:T(8,128)(2,1)}), bf16[16,30,576]{2,1,0:T(8,128)(2,1)}, u32[]{:S(2)}, u32[]{:S(2)}) async-start(bf16[16,30,576]{2,1,0:T(8,128)(2,1)} %broadcast_in_dim.2), calls=%async_computation | async-start | bytes 1310720 | tf_op jit(solution)/shard_map/all_to_all | solution.py:23
  191.6 2.1 convert_element_type.33
  193.7 2.5 copy.11
  196.1 11.7 %all-to-all-done = bf16[16,30,576]{2,1,0:T(8,128)(2,1)} async-done(((bf16[16,30,576]{2,1,0:T(8,128)(2,1)}), bf16[16,30,576]{2,1,0:T(8,128)(2,1)}, u32[]{:S(2)}, u32[]{:S(2)}) %all-to-all-start) | async-done | bytes 552992 | tf_op jit(solution)/shard_map/all_to_all | solution.py:23
  207.9 9.3 %all-to-all-start.1 = ((bf16[30,16,1152]{2,0,1:T(8,128)(2,1)}), bf16[30,16,1152]{2,0,1:T(8,128)(2,1)S(1)}, u32[]{:S(2)}, u32[]{:S(2)}) async-start(bf16[30,16,1152]{2,0,1:T(8,128)(2,1)} %copy.11), calls=%async_computation.1 | async-start | bytes 2359296 | tf_op jit(solution)/shard_map/all_to_all | solution.py:68
  217.2 1.4 reshape.28
  218.5 20.6 %all-to-all-done.1 = bf16[30,16,1152]{2,0,1:T(8,128)(2,1)S(1)} async-done(((bf16[30,16,1152]{2,0,1:T(8,128)(2,1)}), bf16[30,16,1152]{2,0,1:T(8,128)(2,1)S(1)}, u32[]{:S(2)}, u32[]{:S(2)}) %all-to-all-start.1) | async-done | bytes 1105952 | tf_op jit(solution)/shard_map/all_to_all | solution.py:68
  239.1 1.1 reshape.29
  240.3 2.6 fusion.1
  242.9 0.0 copy-start.2
  242.9 1.1 copy-done.2
  244.0 2.1 fusion.2
  246.1 1.4 reshape.30
  247.5 42.5 %all_to_all.25 = bf16[32,15,1152]{2,1,0:T(8,128)(2,1)S(1)} all-to-all(bf16[32,15,1152]{2,1,0:T(8,128)(2,1)S(1)} %reshape.30), channel_id=1, replica_groups=mesh['hid'=32,'col'=16] {'hid'}, dimensions={0} | all-to-all | bytes 2211840 | tf_op jit(solution)/shard_map/all_to_all | solution.py:39
  290.0 0.8 convert_reduce_fusion
Async XLA Ops:
  0.6 1.7 copy-start
  0.6 1.6 copy-start.1
  181.2 26.7 %all-to-all-start = ((bf16[16,30,576]{2,1,0:T(8,128)(2,1)}), bf16[16,30,576]{2,1,0:T(8,128)(2,1)}, u32[]{:S(2)}, u32[]{:S(2)}) async-start(bf16[16,30,576]{2,1,0:T(8,128)(2,1)} %broadcast_in_dim.2), calls=%async_computation | async-start | bytes 1310720 | tf_op jit(solution)/shard_map/all_to_all | solution.py:23
  207.9 31.2 %all-to-all-start.1 = ((bf16[30,16,1152]{2,0,1:T(8,128)(2,1)}), bf16[30,16,1152]{2,0,1:T(8,128)(2,1)S(1)}, u32[]{:S(2)}, u32[]{:S(2)}) async-start(bf16[30,16,1152]{2,0,1:T(8,128)(2,1)} %copy.11), calls=%async_computation.1 | async-start | bytes 2359296 | tf_op jit(solution)/shard_map/all_to_all | solution.py:68
  242.9 1.1 copy-start.2
where the time goes:
time: 292 us; the launch traced here: 291 us
  blocking collectives  212 us (73%)
  waiting for transfers between devices  32.3 us (11%)
  starting transfers between devices  19.7 us (7%)
  local copies, waits for them, and re-layouts  16.2 us (6%)
  matrix products  8.49 us (3%)
    psum x1, blocking collectives, per_device(): feat, grad = lax.psum((feat_part, grad_part), 'hid')  170 us
    all_to_all x1, blocking collectives, sum_at_owner(): lax.all_to_all(pieces, axis, split_axis=0, concat_axis=0, tiled=True)  42.5 us
    all_to_all x1, waiting for transfers between devices, per_device(): lax.all_to_all(own_rows.reshape(own_count, col_count, n_width * POUT), 'c...  20.6 us
    all_to_all x1, waiting for transfers between devices, sent_to_all(): lax.all_to_all(jnp.broadcast_to(value[None], (count, *value.shape)), axis...  11.7 us
    all_to_all x1, starting transfers between devices, sent_to_all(): lax.all_to_all(jnp.broadcast_to(value[None], (count, *value.shape)), axis...  10.5 us
    all_to_all x1, starting transfers between devices, per_device(): lax.all_to_all(own_rows.reshape(own_count, col_count, n_width * POUT), 'c...  9.28 us
    convert_element_type x3, local copies, waits for them, and re-layouts, pair_rows(): return formed.reshape(count, width * POUT).astype(jnp.bfloat16)  7.23 us
  transfers between devices with their start and end apart: 2, of which 2 were waited for; matrix products, arithmetic and copies ran while one was open for 2% of the time, Pallas kernels for 0%

commit v1 on v0

v1 whole, which is shorter than its diff:
```python
import jax
import jax.numpy as jnp
from jax import lax
from jax.experimental import pallas as pl
from jax.experimental.pallas import tpu as pltpu
from jax.sharding import PartitionSpec as P

MESH = pl.DeviceIdType.MESH
F32 = jnp.float32
BF16 = jnp.bfloat16

PIN = 96
POUT = 192
FEATS = PIN + POUT
SEQ = 32
EXAMPLES = 480
NY, NZ = 8, 4
N_HID, N_COL = 32, 16
OWN = 15
TOK = OWN * SEQ
NW = 1152
KW = 576
KP = 640
gram_weight = 1.0 / 64.0
apply_weight = 1.0 / 16.0
NT = (((1,), (1,)), ((), ()))


def slot_of(y, z):
    return (z // 2) * 16 + y * 2 + z % 2


def kernel(
    x_hbm, g_hbm, wi_hbm, wo_hbm, c_hbm,
    app_ref, cn_hbm,
    xv, gv, wiv, wov, cv,
    part, r1, s1, r2, s2, r3, featv, ge, go, rows,
    rn, rk, rkt, cn, p, rp, zs, zr,
    in_sem, a1s, a1r, a2s, a2r, a3s, a3r, ns, nr, ks, kr,
    zas, zar, yas, yar, khs, khr, kxs, kxr, kcs, kcr,
    rps, rpr, zrs, zrr, out_sem,
):
    h = lax.axis_index("hid")
    c = lax.axis_index("col")
    y, z = h // NZ, h % NZ
    core = c % 2
    m = c // 2
    x, zh = m // 2, m % 2
    half = z % 2
    is_target = z == 2 * core + y // 4
    is_root = jnp.logical_and(y == m, core == z // 2)
    own_slot = slot_of(y, z)

    def hid_dev(yy, zz):
        return (yy * NZ + zz, c)

    def col_dev(cc):
        return (h, cc)

    def send(src, dst, ssem, rsem, dev):
        copy = pltpu.make_async_remote_copy(
            src_ref=src, dst_ref=dst, send_sem=ssem, recv_sem=rsem,
            device_id=dev, device_id_type=MESH,
        )
        copy.start()

    def wait_for(ref, sem):
        pltpu.make_async_copy(ref, ref, sem).wait()

    loads = []
    for i, (src, dst) in enumerate(
        ((x_hbm, xv), (wi_hbm, wiv), (g_hbm, gv), (wo_hbm, wov), (c_hbm, cv))
    ):
        load = pltpu.make_async_copy(src, dst, in_sem.at[i])
        load.start()
        loads.append(load)

    barrier = pltpu.get_barrier_semaphore()

    def greet(dev):
        pl.semaphore_signal(barrier, inc=1, device_id=dev, device_id_type=MESH)

    for d in range(1, NY):
        greet(hid_dev((y + d) % NY, z))
    for d in range(1, NZ):
        greet(hid_dev(y, (z + d) % NZ))
    zh_c = (x * 2 + (1 - zh)) * 2 + core
    greet(col_dev(zh_c))
    for d in range(1, 4):
        greet(col_dev((((x + d) % 4) * 2 + zh) * 2 + core))
    greet(col_dev(m * 2 + 1 - core))

    @pl.when(jnp.logical_not(is_root))
    def _():
        greet(col_dev(h // 2))

    zero_tail = jnp.zeros((FEATS, 128), BF16)
    for hf in range(2):
        part[4 * hf + 3] = zero_tail
    loads[2].wait()
    loads[3].wait()

    def project(w, v, first):
        for hf in range(2):
            t = lax.dot_general(
                w[...], v[TOK * hf : TOK * (hf + 1), :], NT, preferred_element_type=F32
            ).astype(BF16)
            n = t.shape[0]
            for q in range(3):
                part[4 * hf + q, first : first + n, :] = t[:, 128 * q : 128 * (q + 1)]
            part[4 * hf + 3, first : first + n, 0:96] = t[:, 384:480]

    project(wov, gv, 0)
    loads[0].wait()
    loads[1].wait()
    project(wiv, xv, POUT)

    pl.semaphore_wait(barrier, jnp.where(is_root, 30, 15))

    for d in (4, 3, 5, 2, 6, 1, 7):
        yy = (y + d) % NY
        send(part.at[yy], r1.at[d - 1], a1s, a1r, hid_dev(yy, z))
    parity_zero = jnp.zeros((64, NW), BF16)
    cn[pl.ds(pl.multiple_of(KW * (1 - h % 2), 64), 64), :] = parity_zero
    wait_for(r1, a1r)
    total = part[y].astype(F32)
    for d in range(7):
        total = total + r1[d].astype(F32)
    s1[...] = total.astype(BF16)

    z_target = 2 * core + y // 4

    @pl.when(jnp.logical_not(is_target))
    def _():
        send(s1, r2.at[(z - z_target + NZ) % NZ - 1], a2s, a2r, hid_dev(y, z_target))
        wait_for(s1, a2s)

    @pl.when(is_target)
    def _():
        wait_for(r2, a2r)
        whole = s1[...].astype(F32)
        for d in range(3):
            whole = whole + r2[d].astype(F32)
        s2[...] = whole.astype(BF16)
        place = r3.at[:, pl.ds(pl.multiple_of(128 * (y % 4), 128), 128)]

        @pl.when(y != m)
        def _():
            send(s2, place, a3s, a3r, hid_dev(m, z))
            wait_for(s2, a3s)

        @pl.when(y == m)
        def _():
            pltpu.make_async_copy(s2, place, a3r).start()

    k_base = core * 16 + m * 2

    @pl.when(is_root)
    def _():
        wait_for(r3, a3r)
        ge[0:POUT, :] = r3[0:POUT, :]
        ge[POUT:256, :] = jnp.zeros((64, 512), BF16)
        go[0:64, :] = jnp.zeros((64, 512), BF16)
        go[64:256, :] = r3[0:POUT, :]
        featv[...] = r3[POUT:FEATS, :].astype(F32)
        mine = (
            lax.broadcasted_iota(jnp.int32, (16, 512), 1) // SEQ
            == lax.broadcasted_iota(jnp.int32, (16, 512), 0)
        )

        def form(i, carry):
            def spread(odd):
                return jnp.concatenate(
                    [
                        jnp.where(
                            mine,
                            jnp.broadcast_to(featv[pl.ds(i * 24 + 2 * q + odd, 1), :], (16, 512)),
                            0.0,
                        ).astype(BF16)
                        for q in range(12)
                    ],
                    axis=0,
                )

            even = lax.dot_general(spread(0), ge[...], NT, preferred_element_type=F32)
            odd = lax.dot_general(spread(1), go[...], NT, preferred_element_type=F32)
            for q in range(12):
                e = even[16 * q : 16 * (q + 1)]
                o = odd[16 * q : 16 * (q + 1)]
                three = jnp.concatenate(
                    [e[:, 0:128], e[:, 128:256] + o[:, 0:128], o[:, 128:256]], axis=1
                )
                at = pl.multiple_of(i * 4608 + 384 * q, 128)
                rows[:, pl.ds(at, 384)] = three.astype(BF16)
            return carry

        lax.fori_loop(0, 4, form, 0)

        def n_slice(cc):
            return rows.at[:, pl.ds(pl.multiple_of(cc * NW, 128), NW)]

        def k_slice(kk):
            return rows.at[:, pl.ds(pl.multiple_of((kk // 2) * NW + (kk % 2) * 512, 128), KP)]

        pltpu.make_async_copy(n_slice(c), rn.at[own_slot], nr).start()
        pltpu.make_async_copy(k_slice(h), rk.at[own_slot], kr).start()

        def to_col(d, carry):
            cc = (c + d) % N_COL
            send(n_slice(cc), rn.at[own_slot], ns, nr, col_dev(cc))
            return carry

        lax.fori_loop(1, N_COL, to_col, 0)

        def to_hid(d, carry):
            kk = (h + d) % N_HID
            send(k_slice(kk), rk.at[own_slot], ks, kr, (kk, c))
            return carry

        lax.fori_loop(1, N_HID, to_hid, 0)

    up, down = (y + 1) % NY, (y + NY - 1) % NY

    def y_block(hop, way, j):
        yy = (y - hop + NY) % NY if way == 0 else (y + hop) % NY
        return rn.at[slot_of(yy, (z + j) % NZ)]

    def y_hops(way, j):
        return 4 if (j < 2) == (way == 0) else 3

    def y_send(hop, way, j):
        block = y_block(hop, way, j)
        send(block, block, yas, yar.at[way, hop, j], hid_dev(up if way == 0 else down, z))

    wait_for(rn.at[own_slot], nr)
    for way in range(2):
        y_send(0, way, 0)
    for d in range(1, NZ):
        send(rn.at[own_slot], rn.at[own_slot], zas, zar.at[NZ - d], hid_dev(y, (z + d) % NZ))
    wait_for(rk.at[pl.ds(k_base, 2)], kr)
    k_two = rk.at[pl.ds(k_base, 2)]
    send(k_two, k_two, khs, khr, col_dev(zh_c))
    for j in range(1, NZ):
        wait_for(rn.at[slot_of(y, (z + j) % NZ)], zar.at[j])
        for way in range(2):
            y_send(0, way, j)
    k_four = rk.at[pl.ds(core * 16 + x * 4, 4)]
    for hop in range(1, 5):
        for j in range(NZ):
            for way in range(2):
                if hop <= y_hops(way, j):
                    wait_for(y_block(hop, way, j), yar.at[way, hop - 1, j])
                    if hop < y_hops(way, j):
                        y_send(hop, way, j)
        if hop == 1:
            wait_for(rk.at[pl.ds(core * 16 + x * 4 + (1 - zh) * 2, 2)], khr)
            for d in range(1, 4):
                xx = (x + d) % 4
                send(k_four, k_four, kxs, kxr.at[d - 1], col_dev((xx * 2 + zh) * 2 + core))
        if hop == 3:
            for d in range(1, 4):
                wait_for(rk.at[pl.ds(core * 16 + ((x + 4 - d) % 4) * 4, 4)], kxr.at[d - 1])
            k_all = rk.at[pl.ds(core * 16, 16)]
            send(k_all, k_all, kcs, kcr, col_dev(m * 2 + 1 - core))
    wait_for(rk.at[pl.ds((1 - core) * 16, 16)], kcr)

    off = 64 * (h % 2)
    rkt[...] = rk[...].reshape(512, KP).T
    loads[4].wait()
    factor = gram_weight / EXAMPLES
    for b in range(3):
        left = rkt[pl.ds(pl.multiple_of(off + 192 * b, 64), 192), :]
        for n in range(3):
            cols = slice(384 * n, 384 * (n + 1))
            gram = jnp.dot(left, rn[:, :, cols].reshape(512, 384), preferred_element_type=F32)
            new = cv[192 * b : 192 * (b + 1), cols].astype(F32) + gram * factor
            cn[pl.ds(pl.multiple_of(off + 192 * b, 64), 192), cols] = new.astype(BF16)
    out = pltpu.make_async_copy(cn.at[pl.ds(pl.multiple_of(off, 64), KW)], cn_hbm, out_sem)
    out.start()

    for b in range(4):
        prod = jnp.dot(
            rk[8 * b : 8 * (b + 1)].reshape(128, KP), cn[...], preferred_element_type=F32
        )
        p[8 * b : 8 * (b + 1)] = (prod * apply_weight).astype(BF16).reshape(8, 16, NW)

    def p_slot(left_hops, way, j):
        yy = (y + left_hops) % NY if way == 0 else (y - left_hops + NY) % NY
        return slot_of(yy, j)

    for step in range(4):
        for j in range(NZ):
            for way in range(2):
                hops = y_hops(way, j)
                left = 4 - step
                if left > hops:
                    continue
                at = p_slot(left, way, j)
                if left == hops:
                    src = p.at[at]
                else:
                    src = rp.at[way, step - 1, j]
                    wait_for(src, rpr.at[way, step - 1, j])
                    src[...] = (src[...].astype(F32) + p[at].astype(F32)).astype(BF16)
                send(src, rp.at[way, step, j], rps, rpr.at[way, step, j],
                     hid_dev(up if way == 0 else down, z))
    for j in range(NZ):
        for way in range(2):
            wait_for(rp.at[way, 3, j], rpr.at[way, 3, j])
        done = p[slot_of(y, j)].astype(F32)
        for way in range(2):
            done = done + rp[way, 3, j].astype(F32)
        zs[j] = done.astype(BF16)

        @pl.when(z != j)
        def _():
            send(zs.at[j], zr.at[(j - z + NZ) % NZ - 1], zrs, zrr, hid_dev(y, j))

    wait_for(zr, zrr)
    final = zs[z].astype(F32)
    for d in range(3):
        final = final + zr[d].astype(F32)
    app_ref[...] = final[0:OWN, :]

    wait_for(r1, a1s)
    wait_for(rn.at[pl.ds(0, 3)], zas)
    wait_for(rn.at[pl.ds(0, 28)], yas)
    wait_for(rk.at[pl.ds(0, 2)], khs)
    wait_for(rk.at[pl.ds(0, 12)], kxs)
    wait_for(rk.at[pl.ds(0, 16)], kcs)
    wait_for(rn.at[pl.ds(0, 28)], rps)
    wait_for(zr, zrs)

    @pl.when(is_root)
    def _():
        wait_for(rn.at[pl.ds(0, 15)], ns)
        wait_for(rk.at[pl.ds(0, 31)], ks)

    out.wait()


def per_device(inputs, out_grads, proj_in, proj_out, curvature):
    dma = pltpu.SemaphoreType.DMA
    vm = pltpu.VMEM
    hbm = pl.BlockSpec(memory_space=pl.ANY)
    return pl.pallas_call(
        kernel,
        out_shape=(
            jax.ShapeDtypeStruct((OWN, NW), F32),
            jax.ShapeDtypeStruct((KW, NW), BF16),
        ),
        in_specs=[hbm] * 5,
        out_specs=(pl.BlockSpec(memory_space=pltpu.VMEM), hbm),
        scratch_shapes=[
            vm(inputs.shape, BF16), vm(out_grads.shape, BF16), vm(proj_in.shape, BF16),
            vm(proj_out.shape, BF16), vm(curvature.shape, BF16),
            vm((8, FEATS, 128), BF16), vm((7, FEATS, 128), BF16), vm((FEATS, 128), BF16),
            vm((3, FEATS, 128), BF16), vm((FEATS, 128), BF16), vm((FEATS, 512), BF16),
            vm((PIN, 512), F32), vm((256, 512), BF16), vm((256, 512), BF16),
            vm((16, PIN * POUT), BF16),
            vm((32, 16, NW), BF16), vm((32, 16, KP), BF16), vm((KP, 512), BF16),
            vm((KP, NW), BF16), vm((32, 16, NW), BF16), vm((2, 4, 4, 16, NW), BF16),
            vm((4, 16, NW), BF16), vm((3, 16, NW), BF16),
            dma((5,)), dma, dma, dma, dma, dma, dma, dma, dma, dma, dma,
            dma, dma((4,)), dma, dma((2, 4, 4)), dma, dma, dma, dma((3,)), dma, dma,
            dma, dma((2, 4, 4)), dma, dma, dma,
        ],
        compiler_params=pltpu.CompilerParams(
            collective_id=0, has_side_effects=True, vmem_limit_bytes=48 * 2**20
        ),
    )(inputs, out_grads, proj_in, proj_out, curvature)


def solution(mesh):
    in_specs = (P("col", "hid"), P("col", "hid"), P(None, "hid"), P(None, "hid"), P("hid", "col"))
    out_specs = (P("hid", "col"), P("hid", "col"))
    return jax.shard_map(
        per_device, mesh=mesh, in_specs=in_specs, out_specs=out_specs, check_vma=False
    )
```

time: 292 us -> 102 us (0.35)
  blocking collectives: 212 us -> 0 us
  Pallas kernels: 0 us -> 93.9 us
  waiting for transfers between devices: 32.3 us -> 0 us
  starting transfers between devices: 19.7 us -> 0 us
  local copies, waits for them, and re-layouts: 16.2 us -> 7.31 us
  matrix products: 8.49 us -> 0 us
    psum x1 -> x0, blocking collectives: 170 us -> none  [per_device(): feat, grad = lax.psum((feat_part, grad_part), 'hid')]
    pallas_call x0 -> x1, Pallas kernels: none -> 93.9 us  [per_device(): pl.pallas_call(kernel, out_shape=(jax.ShapeDtypeStruct((OWN, NW), F32), j...]
    all_to_all x1 -> x0, blocking collectives: 42.5 us -> none  [sum_at_owner(): lax.all_to_all(pieces, axis, split_axis=0, concat_axis=0, tiled=True)]
    all_to_all x2 -> x0, waiting for transfers between devices: 32.3 us -> none  [the longest x1 20.6 us: per_device(): lax.all_to_all(own_rows.reshape(own_count, col_count, n_width * POUT), 'c...]
    all_to_all x2 -> x0, starting transfers between devices: 19.7 us -> none  [the longest x1 10.5 us: sent_to_all(): lax.all_to_all(jnp.broadcast_to(value[None], (count, *value.shape)), axis...]
    convert_element_type x5 -> x0, local copies, waits for them, and re-layouts: 9.33 us -> none  [the longest x3 7.23 us: pair_rows(): return formed.reshape(count, width * POUT).astype(jnp.bfloat16)]
    dot_general x5 -> x0, matrix products: 8.49 us -> none  [the longest x1 2.61 us: per_device(): lax.dot_general(rows_k, rows_n, (((0,), (0,)), ((), ())), preferred_eleme...]
    unnamed x6 -> x12, local copies, waits for them, and re-layouts: 1.21 us -> 7.31 us
  transfers between devices with their start and end apart: 2 -> 0, of which waited for: 2 -> 0; matrix products, arithmetic and copies ran while one was open for 2% -> 0% of each run, Pallas kernels for 0% -> 0%
where the time goes in v1:
time: 102 us
  Pallas kernels  93.9 us (92%)
  local copies, waits for them, and re-layouts  7.31 us (7%)
    pallas_call x1, Pallas kernels, per_device(): pl.pallas_call(kernel, out_shape=(jax.ShapeDtypeStruct((OWN, NW), F32), j...  93.9 us
    unnamed x12, local copies, waits for them, and re-layouts  7.31 us

profile of v1, /device:TPU:6, one launch (start us, length us, event | category | flops | bytes accessed | tf_op | source)
XLA Modules:
  0.0 101.9 jit_solution(7405002718802801760)
XLA Ops:
  0.6 0.0 copy-start
  0.6 1.5 %copy-done = bf16[960,896]{1,0:T(8,128)(2,1)S(1)} copy-done((bf16[960,896]{1,0:T(8,128)(2,1)S(1)}, bf16[960,896]{1,0:T(8,128)(2,1)}, u32[]{:S(2)}) %copy-start) | copy-done | bytes 1720344
  2.1 0.0 copy-start.1
  2.1 1.3 %copy-done.1 = bf16[576,1152]{1,0:T(8,128)(2,1)S(1)} copy-done((bf16[576,1152]{1,0:T(8,128)(2,1)S(1)}, bf16[576,1152]{1,0:T(8,128)(2,1)}, u32[]{:S(2)}) %copy-start.1) | copy-done | bytes 1327128
  3.4 0.0 copy-start.2
  3.4 1.0 %copy-done.2 = bf16[960,256]{1,0:T(8,128)(2,1)S(1)} copy-done((bf16[960,256]{1,0:T(8,128)(2,1)S(1)}, bf16[960,256]{1,0:T(8,128)(2,1)}, u32[]{:S(2)}) %copy-start.2) | copy-done | bytes 491544
  4.4 0.0 copy-start.3
  4.4 0.9 copy-done.3
  5.4 0.0 copy-start.4
  5.4 0.9 copy-done.4
  6.3 93.9 %shard_map.68 = (f32[15,1152]{1,0:T(8,128)S(1)}, bf16[576,1152]{1,0:T(8,128)(2,1)S(1)}) custom-call(bf16[960,896]{1,0:T(8,128)(2,1)S(1)} %copy-done, bf16[960,256]{1,0:T(8,128)(2,1)S(1)} %copy-done.2, bf16[96,896]{1,0:T(8,128)(2,1)S(1)} %copy-done.3, bf16[192,256]{1,0:T(8,128)(2,1)S(1)} %copy-done.4, bf16[576,1152]{1,0:T(8,128)(2,1)S(1)} %copy-done.1), custom_call_target="tpu_custom_call" | custom-call | tf_op jit(solution)/shard_map/pallas_call | solution.py:346
  100.2 0.6 copy.9
  100.8 1.1 %copy.10 = bf16[576,1152]{1,0:T(8,128)(2,1)} copy(bf16[576,1152]{1,0:T(8,128)(2,1)S(1)} %get-tuple-element.5) | data formatting | bytes 2654208
Async XLA Ops:
  0.6 1.5 %copy-start = (bf16[960,896]{1,0:T(8,128)(2,1)S(1)}, bf16[960,896]{1,0:T(8,128)(2,1)}, u32[]{:S(2)}) copy-start(bf16[960,896]{1,0:T(8,128)(2,1)} %x_hbm.1) | copy-start | bytes 5160964
  2.1 1.3 %copy-start.1 = (bf16[576,1152]{1,0:T(8,128)(2,1)S(1)}, bf16[576,1152]{1,0:T(8,128)(2,1)}, u32[]{:S(2)}) copy-start(bf16[576,1152]{1,0:T(8,128)(2,1)} %c_hbm.1) | copy-start | bytes 3981316
  3.4 1.0 %copy-start.2 = (bf16[960,256]{1,0:T(8,128)(2,1)S(1)}, bf16[960,256]{1,0:T(8,128)(2,1)}, u32[]{:S(2)}) copy-start(bf16[960,256]{1,0:T(8,128)(2,1)} %g_hbm.1) | copy-start | bytes 1474564
  4.4 0.9 copy-start.3
  5.4 0.9 copy-start.4

commit v2 on v1

--- a/solution.py
+++ b/solution.py
@@ -28,6 +28,14 @@
 
 def slot_of(y, z):
     return (z // 2) * 16 + y * 2 + z % 2
+
+
+def root_group(y, z):
+    return (y + 16 - 4 * (z % 2) - 2 * (z // 2)) % NY
+
+
+def block_slot(y, z):
+    return slot_of(root_group(y, z), z)
 
 
 def kernel(
@@ -46,10 +54,16 @@
     core = c % 2
     m = c // 2
     x, zh = m // 2, m % 2
-    half = z % 2
-    is_target = z == 2 * core + y // 4
-    is_root = jnp.logical_and(y == m, core == z // 2)
-    own_slot = slot_of(y, z)
+    first_y = (m + 2 * core + NY - 1) % NY
+
+    def chunk_of(yy):
+        return (yy + NY - first_y) % NY
+
+    z_target = 2 * core + chunk_of(y) // 4
+    y_root = (m + 4 * (z % 2) + 2 * (z // 2)) % NY
+    is_target = z == z_target
+    is_root = jnp.logical_and(y == y_root, core == z // 2)
+    own_slot = block_slot(y, z)
 
     def hid_dev(yy, zz):
         return (yy * NZ + zz, c)
@@ -92,7 +106,7 @@
 
     @pl.when(jnp.logical_not(is_root))
     def _():
-        greet(col_dev(h // 2))
+        greet(col_dev(root_group(y, z) * 2 + z // 2))
 
     zero_tail = jnp.zeros((FEATS, 128), BF16)
     for hf in range(2):
@@ -119,16 +133,15 @@
 
     for d in (4, 3, 5, 2, 6, 1, 7):
         yy = (y + d) % NY
-        send(part.at[yy], r1.at[d - 1], a1s, a1r, hid_dev(yy, z))
+        send(part.at[chunk_of(yy)], r1.at[d - 1], a1s, a1r, hid_dev(yy, z))
     parity_zero = jnp.zeros((64, NW), BF16)
     cn[pl.ds(pl.multiple_of(KW * (1 - h % 2), 64), 64), :] = parity_zero
     wait_for(r1, a1r)
-    total = part[y].astype(F32)
+    total = part[chunk_of(y)].astype(F32)
     for d in range(7):
         total = total + r1[d].astype(F32)
     s1[...] = total.astype(BF16)
 
-    z_target = 2 * core + y // 4
 
     @pl.when(jnp.logical_not(is_target))
     def _():
@@ -142,14 +155,14 @@
         for d in range(3):
             whole = whole + r2[d].astype(F32)
         s2[...] = whole.astype(BF16)
-        place = r3.at[:, pl.ds(pl.multiple_of(128 * (y % 4), 128), 128)]
-
-        @pl.when(y != m)
+        place = r3.at[:, pl.ds(pl.multiple_of(128 * (chunk_of(y) % 4), 128), 128)]
+
+        @pl.when(y != y_root)
         def _():
-            send(s2, place, a3s, a3r, hid_dev(m, z))
+            send(s2, place, a3s, a3r, hid_dev(y_root, z))
             wait_for(s2, a3s)
 
-        @pl.when(y == m)
+        @pl.when(y == y_root)
         def _():
             pltpu.make_async_copy(s2, place, a3r).start()
 
@@ -223,7 +236,7 @@
 
     def y_block(hop, way, j):
         yy = (y - hop + NY) % NY if way == 0 else (y + hop) % NY
-        return rn.at[slot_of(yy, (z + j) % NZ)]
+        return rn.at[block_slot(yy, (z + j) % NZ)]
 
     def y_hops(way, j):
         return 4 if (j < 2) == (way == 0) else 3
@@ -241,7 +254,7 @@
     k_two = rk.at[pl.ds(k_base, 2)]
     send(k_two, k_two, khs, khr, col_dev(zh_c))
     for j in range(1, NZ):
-        wait_for(rn.at[slot_of(y, (z + j) % NZ)], zar.at[j])
+        wait_for(rn.at[block_slot(y, (z + j) % NZ)], zar.at[j])
         for way in range(2):
             y_send(0, way, j)
     k_four = rk.at[pl.ds(core * 16 + x * 4, 4)]
@@ -366,7 +379,7 @@
             dma, dma((2, 4, 4)), dma, dma, dma,
         ],
         compiler_params=pltpu.CompilerParams(
-            collective_id=0, has_side_effects=True, vmem_limit_bytes=48 * 2**20
+            collective_id=0, has_side_effects=True, vmem_limit_bytes=60 * 2**20
         ),
     )(inputs, out_grads, proj_in, proj_out, curvature)
 

time: 102 us -> 96.1 us (0.942)
  local copies, waits for them, and re-layouts: 7.31 us -> 4.01 us
  Pallas kernels: 93.9 us -> 91 us
    unnamed x12 -> x2, local copies, waits for them, and re-layouts: 7.31 us -> 4.01 us
    pallas_call x1, Pallas kernels: 93.9 us -> 91 us  [per_device(): pl.pallas_call(kernel, out_shape=(jax.ShapeDtypeStruct((OWN, NW), F32), j...]
where the time goes in v2:
time: 96.1 us; the launch traced here: 95.6 us
  Pallas kernels  91 us (95%)
  local copies, waits for them, and re-layouts  4.01 us (4%)
    pallas_call x1, Pallas kernels, per_device(): pl.pallas_call(kernel, out_shape=(jax.ShapeDtypeStruct((OWN, NW), F32), j...  91 us
    unnamed x2, local copies, waits for them, and re-layouts  4.01 us

profile of v2, /device:TPU:6, one launch (start us, length us, event | category | flops | bytes accessed | tf_op | source)
XLA Modules:
  0.0 95.6 jit_solution(8820376948965917354)
XLA Ops:
  0.6 91.0 %shard_map.68 = (f32[15,1152]{1,0:T(8,128)}, bf16[576,1152]{1,0:T(8,128)(2,1)}) custom-call(bf16[960,896]{1,0:T(8,128)(2,1)} %x_hbm.1, bf16[960,256]{1,0:T(8,128)(2,1)} %g_hbm.1, bf16[96,896]{1,0:T(8,128)(2,1)} %wi_hbm.1, bf16[192,256]{1,0:T(8,128)(2,1)} %wo_hbm.1, bf16[576,1152]{1,0:T(8,128)(2,1)} %c_hbm.1), custom_call_target="tpu_custom_call" | custom-call | tf_op jit(solution)/shard_map/pallas_call | solution.py:359
  91.6 1.5 %copy.9 = f32[15,1152]{1,0:T(8,128)} copy(f32[15,1152]{1,0:T(8,128)} %get-tuple-element.4) | data formatting | bytes 138240
  93.1 2.5 %copy.10 = bf16[576,1152]{1,0:T(8,128)(2,1)} copy(bf16[576,1152]{1,0:T(8,128)(2,1)} %get-tuple-element.5) | data formatting | bytes 2654208

commit v3 on v2

--- a/solution.py
+++ b/solution.py
@@ -41,12 +41,12 @@
 def kernel(
     x_hbm, g_hbm, wi_hbm, wo_hbm, c_hbm,
     app_ref, cn_hbm,
-    xv, gv, wiv, wov, cv,
+    xv, gv, wiv, wov, cx,
     part, r1, s1, r2, s2, r3, featv, ge, go, rows,
-    rn, rk, rkt, cn, p, rp, zs, zr,
+    rn, rk, rkt, cn, p, rp, zs, zr, sp, sq, sr, sall,
     in_sem, a1s, a1r, a2s, a2r, a3s, a3r, ns, nr, ks, kr,
     zas, zar, yas, yar, khs, khr, kxs, kxr, kcs, kcr,
-    rps, rpr, zrs, zrr, out_sem,
+    rps, rpr, zrs, zrr, scs, scr, sms, smr, out_sem,
 ):
     h = lax.axis_index("hid")
     c = lax.axis_index("col")
@@ -81,9 +81,13 @@
     def wait_for(ref, sem):
         pltpu.make_async_copy(ref, ref, sem).wait()
 
+    off = pl.multiple_of(64 * (h % 2), 64)
     loads = []
     for i, (src, dst) in enumerate(
-        ((x_hbm, xv), (wi_hbm, wiv), (g_hbm, gv), (wo_hbm, wov), (c_hbm, cv))
+        (
+            (x_hbm, xv), (wi_hbm, wiv), (g_hbm, gv), (wo_hbm, wov),
+            (c_hbm, cx.at[pl.ds(off, KW)]),
+        )
     ):
         load = pltpu.make_async_copy(src, dst, in_sem.at[i])
         load.start()
@@ -134,8 +138,7 @@
     for d in (4, 3, 5, 2, 6, 1, 7):
         yy = (y + d) % NY
         send(part.at[chunk_of(yy)], r1.at[d - 1], a1s, a1r, hid_dev(yy, z))
-    parity_zero = jnp.zeros((64, NW), BF16)
-    cn[pl.ds(pl.multiple_of(KW * (1 - h % 2), 64), 64), :] = parity_zero
+    cx[pl.ds(pl.multiple_of(KW * (1 - h % 2), 64), 64), :] = jnp.zeros((64, NW), BF16)
     wait_for(r1, a1r)
     total = part[chunk_of(y)].astype(F32)
     for d in range(7):
@@ -257,51 +260,20 @@
         wait_for(rn.at[block_slot(y, (z + j) % NZ)], zar.at[j])
         for way in range(2):
             y_send(0, way, j)
-    k_four = rk.at[pl.ds(core * 16 + x * 4, 4)]
-    for hop in range(1, 5):
+
+    def y_round(hop):
         for j in range(NZ):
             for way in range(2):
                 if hop <= y_hops(way, j):
                     wait_for(y_block(hop, way, j), yar.at[way, hop - 1, j])
                     if hop < y_hops(way, j):
                         y_send(hop, way, j)
-        if hop == 1:
-            wait_for(rk.at[pl.ds(core * 16 + x * 4 + (1 - zh) * 2, 2)], khr)
-            for d in range(1, 4):
-                xx = (x + d) % 4
-                send(k_four, k_four, kxs, kxr.at[d - 1], col_dev((xx * 2 + zh) * 2 + core))
-        if hop == 3:
-            for d in range(1, 4):
-                wait_for(rk.at[pl.ds(core * 16 + ((x + 4 - d) % 4) * 4, 4)], kxr.at[d - 1])
-            k_all = rk.at[pl.ds(core * 16, 16)]
-            send(k_all, k_all, kcs, kcr, col_dev(m * 2 + 1 - core))
-    wait_for(rk.at[pl.ds((1 - core) * 16, 16)], kcr)
-
-    off = 64 * (h % 2)
-    rkt[...] = rk[...].reshape(512, KP).T
-    loads[4].wait()
-    factor = gram_weight / EXAMPLES
-    for b in range(3):
-        left = rkt[pl.ds(pl.multiple_of(off + 192 * b, 64), 192), :]
-        for n in range(3):
-            cols = slice(384 * n, 384 * (n + 1))
-            gram = jnp.dot(left, rn[:, :, cols].reshape(512, 384), preferred_element_type=F32)
-            new = cv[192 * b : 192 * (b + 1), cols].astype(F32) + gram * factor
-            cn[pl.ds(pl.multiple_of(off + 192 * b, 64), 192), cols] = new.astype(BF16)
-    out = pltpu.make_async_copy(cn.at[pl.ds(pl.multiple_of(off, 64), KW)], cn_hbm, out_sem)
-    out.start()
-
-    for b in range(4):
-        prod = jnp.dot(
-            rk[8 * b : 8 * (b + 1)].reshape(128, KP), cn[...], preferred_element_type=F32
-        )
-        p[8 * b : 8 * (b + 1)] = (prod * apply_weight).astype(BF16).reshape(8, 16, NW)
 
     def p_slot(left_hops, way, j):
         yy = (y + left_hops) % NY if way == 0 else (y - left_hops + NY) % NY
         return slot_of(yy, j)
 
-    for step in range(4):
+    def p_round(step):
         for j in range(NZ):
             for way in range(2):
                 hops = y_hops(way, j)
@@ -317,6 +289,54 @@
                     src[...] = (src[...].astype(F32) + p[at].astype(F32)).astype(BF16)
                 send(src, rp.at[way, step, j], rps, rpr.at[way, step, j],
                      hid_dev(up if way == 0 else down, z))
+
+    wait_for(rk.at[pl.ds(core * 16 + x * 4 + (1 - zh) * 2, 2)], khr)
+    k_four = rk.at[pl.ds(core * 16 + x * 4, 4)]
+    for d in range(1, 4):
+        xx = (x + d) % 4
+        send(k_four, k_four, kxs, kxr.at[d - 1], col_dev((xx * 2 + zh) * 2 + core))
+    y_round(1)
+    for d in range(1, 4):
+        wait_for(rk.at[pl.ds(core * 16 + ((x + 4 - d) % 4) * 4, 4)], kxr.at[d - 1])
+    k_all = rk.at[pl.ds(core * 16, 16)]
+    send(k_all, k_all, kcs, kcr, col_dev(m * 2 + 1 - core))
+    y_round(2)
+    wait_for(rk.at[pl.ds((1 - core) * 16, 16)], kcr)
+    loads[4].wait()
+    for b in range(4):
+        prod = jnp.dot(
+            rk[8 * b : 8 * (b + 1)].reshape(128, KP), cx[...], preferred_element_type=F32
+        )
+        p[8 * b : 8 * (b + 1)] = (prod * apply_weight).astype(BF16).reshape(8, 16, NW)
+    p_round(0)
+    y_round(3)
+    p_round(1)
+    y_round(4)
+
+    sp[...] = lax.dot_general(
+        rn[slot_of(y, z)], rn[...].reshape(512, NW), NT, preferred_element_type=F32
+    ).astype(BF16)
+    send(sp, sq, scs, scr, col_dev(m * 2 + 1 - core))
+    p_round(2)
+    wait_for(sq, scr)
+    sall[...] = (sp[...].astype(F32) + sq[...].astype(F32)).astype(BF16)
+    for d in range(1, 8):
+        send(sall, sr.at[d - 1], sms, smr, col_dev(((m + d) % 8) * 2 + core))
+
+    rkt[...] = rk[...].reshape(512, KP).T
+    factor = gram_weight / EXAMPLES
+    for b in range(3):
+        lines = pl.ds(pl.multiple_of(off + 192 * b, 64), 192)
+        left = rkt[lines, :]
+        for n in range(3):
+            cols = slice(384 * n, 384 * (n + 1))
+            gram = jnp.dot(left, rn[:, :, cols].reshape(512, 384), preferred_element_type=F32)
+            new = cx[lines, cols].astype(F32) + gram * factor
+            cn[192 * b : 192 * (b + 1), cols] = new.astype(BF16)
+    out = pltpu.make_async_copy(cn, cn_hbm, out_sem)
+    out.start()
+
+    p_round(3)
     for j in range(NZ):
         for way in range(2):
             wait_for(rp.at[way, 3, j], rpr.at[way, 3, j])
@@ -329,8 +349,18 @@
         def _():
             send(zs.at[j], zr.at[(j - z + NZ) % NZ - 1], zrs, zrr, hid_dev(y, j))
 
+    wait_for(sr, smr)
+    s = sall[...].astype(F32)
+    for d in range(7):
+        s = s + sr[d].astype(F32)
+    high = s.astype(BF16)
+    low = (s - high.astype(F32)).astype(BF16)
+    both = jnp.dot(
+        jnp.concatenate([high, low], axis=0), rn[...].reshape(512, NW),
+        preferred_element_type=F32,
+    )
+    final = (both[0:16] + both[16:32]) * (factor * apply_weight) + zs[z].astype(F32)
     wait_for(zr, zrr)
-    final = zs[z].astype(F32)
     for d in range(3):
         final = final + zr[d].astype(F32)
     app_ref[...] = final[0:OWN, :]
@@ -343,6 +373,8 @@
     wait_for(rk.at[pl.ds(0, 16)], kcs)
     wait_for(rn.at[pl.ds(0, 28)], rps)
     wait_for(zr, zrs)
+    wait_for(sp, scs)
+    wait_for(sr, sms)
 
     @pl.when(is_root)
     def _():
@@ -366,17 +398,18 @@
         out_specs=(pl.BlockSpec(memory_space=pltpu.VMEM), hbm),
         scratch_shapes=[
             vm(inputs.shape, BF16), vm(out_grads.shape, BF16), vm(proj_in.shape, BF16),
-            vm(proj_out.shape, BF16), vm(curvature.shape, BF16),
+            vm(proj_out.shape, BF16), vm((KP, NW), BF16),
             vm((8, FEATS, 128), BF16), vm((7, FEATS, 128), BF16), vm((FEATS, 128), BF16),
             vm((3, FEATS, 128), BF16), vm((FEATS, 128), BF16), vm((FEATS, 512), BF16),
             vm((PIN, 512), F32), vm((256, 512), BF16), vm((256, 512), BF16),
             vm((16, PIN * POUT), BF16),
             vm((32, 16, NW), BF16), vm((32, 16, KP), BF16), vm((KP, 512), BF16),
-            vm((KP, NW), BF16), vm((32, 16, NW), BF16), vm((2, 4, 4, 16, NW), BF16),
+            vm((KW, NW), BF16), vm((32, 16, NW), BF16), vm((2, 4, 4, 16, NW), BF16),
             vm((4, 16, NW), BF16), vm((3, 16, NW), BF16),
+            vm((16, 512), BF16), vm((16, 512), BF16), vm((7, 16, 512), BF16), vm((16, 512), BF16),
             dma((5,)), dma, dma, dma, dma, dma, dma, dma, dma, dma, dma,
             dma, dma((4,)), dma, dma((2, 4, 4)), dma, dma, dma, dma((3,)), dma, dma,
-            dma, dma((2, 4, 4)), dma, dma, dma,
+            dma, dma((2, 4, 4)), dma, dma, dma, dma, dma, dma, dma,
         ],
         compiler_params=pltpu.CompilerParams(
             collective_id=0, has_side_effects=True, vmem_limit_bytes=60 * 2**20

time: 96.1 us -> 89.3 us (0.929)
  Pallas kernels: 91 us -> 83.9 us
    pallas_call x1, Pallas kernels: 91 us -> 83.9 us  [per_device(): pl.pallas_call(kernel, out_shape=(jax.ShapeDtypeStruct((OWN, NW), F32), j...]
where the time goes in v3:
time: 89.3 us; the launch traced here: 88.5 us
  Pallas kernels  83.9 us (94%)
  local copies, waits for them, and re-layouts  4.01 us (4%)
    pallas_call x1, Pallas kernels, per_device(): pl.pallas_call(kernel, out_shape=(jax.ShapeDtypeStruct((OWN, NW), F32), j...  83.9 us
    unnamed x2, local copies, waits for them, and re-layouts  4.01 us

profile of v3, /device:TPU:6, one launch (start us, length us, event | category | flops | bytes accessed | tf_op | source)
XLA Modules:
  0.0 88.5 jit_solution(4608574716822554884)
XLA Ops:
  0.6 83.9 %shard_map.68 = (f32[15,1152]{1,0:T(8,128)}, bf16[576,1152]{1,0:T(8,128)(2,1)}) custom-call(bf16[960,896]{1,0:T(8,128)(2,1)} %x_hbm.1, bf16[960,256]{1,0:T(8,128)(2,1)} %g_hbm.1, bf16[96,896]{1,0:T(8,128)(2,1)} %wi_hbm.1, bf16[192,256]{1,0:T(8,128)(2,1)} %wo_hbm.1, bf16[576,1152]{1,0:T(8,128)(2,1)} %c_hbm.1), custom_call_target="tpu_custom_call" | custom-call | tf_op jit(solution)/shard_map/pallas_call | solution.py:391
  84.5 1.5 %copy.9 = f32[15,1152]{1,0:T(8,128)} copy(f32[15,1152]{1,0:T(8,128)} %get-tuple-element.4) | data formatting | bytes 138240
  86.0 2.5 %copy.10 = bf16[576,1152]{1,0:T(8,128)(2,1)} copy(bf16[576,1152]{1,0:T(8,128)(2,1)} %get-tuple-element.5) | data formatting | bytes 2654208

commit v4 on v3

--- a/solution.py
+++ b/solution.py
@@ -12,6 +12,8 @@
 PIN = 96
 POUT = 192
 FEATS = PIN + POUT
+ZR = 96
+YR = FEATS - ZR
 SEQ = 32
 EXAMPLES = 480
 NY, NZ = 8, 4
@@ -42,9 +44,9 @@
     x_hbm, g_hbm, wi_hbm, wo_hbm, c_hbm,
     app_ref, cn_hbm,
     xv, gv, wiv, wov, cx,
-    part, r1, s1, r2, s2, r3, featv, ge, go, rows,
+    part, q1, qs, q2, r1, s1, r2, s2, r3, featv, ge, go, rows,
     rn, rk, rkt, cn, p, rp, zs, zr, sp, sq, sr, sall,
-    in_sem, a1s, a1r, a2s, a2r, a3s, a3r, ns, nr, ks, kr,
+    in_sem, q1s, q1r, q2s, q2r, a1s, a1r, a2s, a2r, a3s, a3r, ns, nr, ks, kr,
     zas, zar, yas, yar, khs, khr, kxs, kxr, kcs, kcr,
     rps, rpr, zrs, zrr, scs, scr, sms, smr, out_sem,
 ):
@@ -135,16 +137,39 @@
 
     pl.semaphore_wait(barrier, jnp.where(is_root, 30, 15))
 
+    z_first = pl.ds(0, ZR)
+    y_first = pl.ds(ZR, YR)
+    for d in (2, 1, 3):
+        zz = (z + d) % NZ
+        send(part.at[pl.ds(2 * zz, 2), z_first], q1.at[d - 1], q1s, q1r, hid_dev(y, zz))
     for d in (4, 3, 5, 2, 6, 1, 7):
         yy = (y + d) % NY
-        send(part.at[chunk_of(yy)], r1.at[d - 1], a1s, a1r, hid_dev(yy, z))
+        send(part.at[chunk_of(yy), y_first], r1.at[d - 1], a1s, a1r, hid_dev(yy, z))
     cx[pl.ds(pl.multiple_of(KW * (1 - h % 2), 64), 64), :] = jnp.zeros((64, NW), BF16)
+
+    wait_for(q1, q1r)
+    both = part[pl.ds(2 * z, 2), 0:ZR].astype(F32)
+    for d in range(3):
+        both = both + q1[d].astype(F32)
+    qs[...] = both.astype(BF16)
+    q_z = 2 * core + z // 2
+    q_y = (m + 4 * (z // 2) + 2 * core) % NY
+    q_place = q2.at[y, pl.ds(2 * (z % 2), 2)]
+    q_here = jnp.logical_and(q_y == y, q_z == z)
+
+    @pl.when(q_here)
+    def _():
+        pltpu.make_async_copy(qs, q_place, q2r).start()
+
+    @pl.when(jnp.logical_not(q_here))
+    def _():
+        send(qs, q_place, q2s, q2r, hid_dev(q_y, q_z))
+
     wait_for(r1, a1r)
-    total = part[chunk_of(y)].astype(F32)
+    total = part[chunk_of(y), ZR:FEATS].astype(F32)
     for d in range(7):
         total = total + r1[d].astype(F32)
     s1[...] = total.astype(BF16)
-
 
     @pl.when(jnp.logical_not(is_target))
     def _():
@@ -158,7 +183,7 @@
         for d in range(3):
             whole = whole + r2[d].astype(F32)
         s2[...] = whole.astype(BF16)
-        place = r3.at[:, pl.ds(pl.multiple_of(128 * (chunk_of(y) % 4), 128), 128)]
+        place = r3.at[y_first, pl.ds(pl.multiple_of(128 * (chunk_of(y) % 4), 128), 128)]
 
         @pl.when(y != y_root)
         def _():
@@ -169,11 +194,21 @@
         def _():
             pltpu.make_async_copy(s2, place, a3r).start()
 
+    @pl.when(jnp.logical_not(q_here))
+    def _():
+        wait_for(qs, q2s)
+
     k_base = core * 16 + m * 2
 
     @pl.when(is_root)
     def _():
-        wait_for(r3, a3r)
+        wait_for(q2, q2r)
+        for t in range(4):
+            summed = q2[0, t].astype(F32)
+            for d in range(1, NY):
+                summed = summed + q2[d, t].astype(F32)
+            r3[0:ZR, 128 * t : 128 * (t + 1)] = summed.astype(BF16)
+        wait_for(r3.at[y_first], a3r)
         ge[0:POUT, :] = r3[0:POUT, :]
         ge[POUT:256, :] = jnp.zeros((64, 512), BF16)
         go[0:64, :] = jnp.zeros((64, 512), BF16)
@@ -365,6 +400,7 @@
         final = final + zr[d].astype(F32)
     app_ref[...] = final[0:OWN, :]
 
+    wait_for(q1, q1s)
     wait_for(r1, a1s)
     wait_for(rn.at[pl.ds(0, 3)], zas)
     wait_for(rn.at[pl.ds(0, 28)], yas)
@@ -399,15 +435,16 @@
         scratch_shapes=[
             vm(inputs.shape, BF16), vm(out_grads.shape, BF16), vm(proj_in.shape, BF16),
             vm(proj_out.shape, BF16), vm((KP, NW), BF16),
-            vm((8, FEATS, 128), BF16), vm((7, FEATS, 128), BF16), vm((FEATS, 128), BF16),
-            vm((3, FEATS, 128), BF16), vm((FEATS, 128), BF16), vm((FEATS, 512), BF16),
+            vm((8, FEATS, 128), BF16), vm((3, 2, ZR, 128), BF16), vm((2, ZR, 128), BF16),
+            vm((NY, 4, ZR, 128), BF16), vm((7, YR, 128), BF16), vm((YR, 128), BF16),
+            vm((3, YR, 128), BF16), vm((YR, 128), BF16), vm((FEATS, 512), BF16),
             vm((PIN, 512), F32), vm((256, 512), BF16), vm((256, 512), BF16),
             vm((16, PIN * POUT), BF16),
             vm((32, 16, NW), BF16), vm((32, 16, KP), BF16), vm((KP, 512), BF16),
             vm((KW, NW), BF16), vm((32, 16, NW), BF16), vm((2, 4, 4, 16, NW), BF16),
             vm((4, 16, NW), BF16), vm((3, 16, NW), BF16),
             vm((16, 512), BF16), vm((16, 512), BF16), vm((7, 16, 512), BF16), vm((16, 512), BF16),
-            dma((5,)), dma, dma, dma, dma, dma, dma, dma, dma, dma, dma,
+            dma((5,)), dma, dma, dma, dma, dma, dma, dma, dma, dma, dma, dma, dma, dma, dma,
             dma, dma((4,)), dma, dma((2, 4, 4)), dma, dma, dma, dma((3,)), dma, dma,
             dma, dma((2, 4, 4)), dma, dma, dma, dma, dma, dma, dma,
         ],

time: 89.3 us -> 84.8 us (0.950)
  Pallas kernels: 83.9 us -> 79.4 us
    pallas_call x1, Pallas kernels: 83.9 us -> 79.4 us  [per_device(): pl.pallas_call(kernel, out_shape=(jax.ShapeDtypeStruct((OWN, NW), F32), j...]
where the time goes in v4:
time: 84.8 us; the launch traced here: 84 us
  Pallas kernels  79.4 us (94%)
  local copies, waits for them, and re-layouts  4.01 us (5%)
    pallas_call x1, Pallas kernels, per_device(): pl.pallas_call(kernel, out_shape=(jax.ShapeDtypeStruct((OWN, NW), F32), j...  79.4 us
    unnamed x2, local copies, waits for them, and re-layouts  4.01 us

profile of v4, /device:TPU:6, one launch (start us, length us, event | category | flops | bytes accessed | tf_op | source)
XLA Modules:
  0.0 84.0 jit_solution(7159865840483229274)
XLA Ops:
  0.6 79.4 %shard_map.68 = (f32[15,1152]{1,0:T(8,128)}, bf16[576,1152]{1,0:T(8,128)(2,1)}) custom-call(bf16[960,896]{1,0:T(8,128)(2,1)} %x_hbm.1, bf16[960,256]{1,0:T(8,128)(2,1)} %g_hbm.1, bf16[96,896]{1,0:T(8,128)(2,1)} %wi_hbm.1, bf16[192,256]{1,0:T(8,128)(2,1)} %wo_hbm.1, bf16[576,1152]{1,0:T(8,128)(2,1)} %c_hbm.1), custom_call_target="tpu_custom_call" | custom-call | tf_op jit(solution)/shard_map/pallas_call | solution.py:427
  80.0 1.5 %copy.9 = f32[15,1152]{1,0:T(8,128)} copy(f32[15,1152]{1,0:T(8,128)} %get-tuple-element.4) | data formatting | bytes 138240
  81.5 2.5 %copy.10 = bf16[576,1152]{1,0:T(8,128)(2,1)} copy(bf16[576,1152]{1,0:T(8,128)(2,1)} %get-tuple-element.5) | data formatting | bytes 2654208

commit v5 on v4

--- a/solution.py
+++ b/solution.py
@@ -42,13 +42,13 @@
 
 def kernel(
     x_hbm, g_hbm, wi_hbm, wo_hbm, c_hbm,
-    app_ref, cn_hbm,
+    app_ref, cn_out,
     xv, gv, wiv, wov, cx,
     part, q1, qs, q2, r1, s1, r2, s2, r3, featv, ge, go, rows,
-    rn, rk, rkt, cn, p, rp, zs, zr, sp, sq, sr, sall,
+    rn, rk, rkt, p, rp, zs, zr, sp, sq, sr, sall,
     in_sem, q1s, q1r, q2s, q2r, a1s, a1r, a2s, a2r, a3s, a3r, ns, nr, ks, kr,
     zas, zar, yas, yar, khs, khr, kxs, kxr, kcs, kcr,
-    rps, rpr, zrs, zrr, scs, scr, sms, smr, out_sem,
+    rps, rpr, zrs, zrr, scs, scr, sms, smr,
 ):
     h = lax.axis_index("hid")
     c = lax.axis_index("col")
@@ -256,19 +256,25 @@
         pltpu.make_async_copy(n_slice(c), rn.at[own_slot], nr).start()
         pltpu.make_async_copy(k_slice(h), rk.at[own_slot], kr).start()
 
-        def to_col(d, carry):
-            cc = (c + d) % N_COL
+        def to_col(dx, dz, dc):
+            cc = (((x + dx) % 4) * 2 + (zh + dz) % 2) * 2 + (core + dc) % 2
             send(n_slice(cc), rn.at[own_slot], ns, nr, col_dev(cc))
-            return carry
-
-        lax.fori_loop(1, N_COL, to_col, 0)
-
-        def to_hid(d, carry):
-            kk = (h + d) % N_HID
+
+        def to_hid(dy, dz):
+            kk = ((y + dy) % NY) * NZ + (z + dz) % NZ
             send(k_slice(kk), rk.at[own_slot], ks, kr, (kk, c))
-            return carry
-
-        lax.fori_loop(1, N_HID, to_hid, 0)
+
+        for dx in (2, 1, 3, 0):
+            for dc in range(2):
+                to_col(dx, 1, dc)
+        for dy in (4, 3, 5, 2, 6, 1, 7, 0):
+            for dz in range(NZ):
+                if dy + dz > 0:
+                    to_hid(dy, dz)
+        for dx in (2, 1, 3, 0):
+            for dc in range(2):
+                if dx + dc > 0:
+                    to_col(dx, 0, dc)
 
     up, down = (y + 1) % NY, (y + NY - 1) % NY
 
@@ -306,10 +312,10 @@
 
     def p_slot(left_hops, way, j):
         yy = (y + left_hops) % NY if way == 0 else (y - left_hops + NY) % NY
-        return slot_of(yy, j)
-
-    def p_round(step):
-        for j in range(NZ):
+        return slot_of(yy, (2 * core + j) % NZ)
+
+    def p_round(step, which=range(NZ)):
+        for j in which:
             for way in range(2):
                 hops = y_hops(way, j)
                 left = 4 - step
@@ -336,14 +342,21 @@
     k_all = rk.at[pl.ds(core * 16, 16)]
     send(k_all, k_all, kcs, kcr, col_dev(m * 2 + 1 - core))
     y_round(2)
+    loads[4].wait()
+
+    def product(half):
+        for b in range(2):
+            at = pl.ds(half * 16 + 8 * b, 8)
+            prod = jnp.dot(
+                rk[at].reshape(128, KP), cx[...], preferred_element_type=F32
+            )
+            p[at] = (prod * apply_weight).astype(BF16).reshape(8, 16, NW)
+
+    product(core)
+    p_round(0, (0, 1))
     wait_for(rk.at[pl.ds((1 - core) * 16, 16)], kcr)
-    loads[4].wait()
-    for b in range(4):
-        prod = jnp.dot(
-            rk[8 * b : 8 * (b + 1)].reshape(128, KP), cx[...], preferred_element_type=F32
-        )
-        p[8 * b : 8 * (b + 1)] = (prod * apply_weight).astype(BF16).reshape(8, 16, NW)
-    p_round(0)
+    product(1 - core)
+    p_round(0, (2, 3))
     y_round(3)
     p_round(1)
     y_round(4)
@@ -358,6 +371,8 @@
     for d in range(1, 8):
         send(sall, sr.at[d - 1], sms, smr, col_dev(((m + d) % 8) * 2 + core))
 
+    p_round(3)
+
     rkt[...] = rk[...].reshape(512, KP).T
     factor = gram_weight / EXAMPLES
     for b in range(3):
@@ -367,22 +382,20 @@
             cols = slice(384 * n, 384 * (n + 1))
             gram = jnp.dot(left, rn[:, :, cols].reshape(512, 384), preferred_element_type=F32)
             new = cx[lines, cols].astype(F32) + gram * factor
-            cn[192 * b : 192 * (b + 1), cols] = new.astype(BF16)
-    out = pltpu.make_async_copy(cn, cn_hbm, out_sem)
-    out.start()
-
-    p_round(3)
+            cn_out[192 * b : 192 * (b + 1), cols] = new.astype(BF16)
+
     for j in range(NZ):
+        zz = (2 * core + j) % NZ
         for way in range(2):
             wait_for(rp.at[way, 3, j], rpr.at[way, 3, j])
-        done = p[slot_of(y, j)].astype(F32)
+        done = p[slot_of(y, zz)].astype(F32)
         for way in range(2):
             done = done + rp[way, 3, j].astype(F32)
         zs[j] = done.astype(BF16)
 
-        @pl.when(z != j)
+        @pl.when(z != zz)
         def _():
-            send(zs.at[j], zr.at[(j - z + NZ) % NZ - 1], zrs, zrr, hid_dev(y, j))
+            send(zs.at[j], zr.at[(zz - z + NZ) % NZ - 1], zrs, zrr, hid_dev(y, zz))
 
     wait_for(sr, smr)
     s = sall[...].astype(F32)
@@ -394,7 +407,7 @@
         jnp.concatenate([high, low], axis=0), rn[...].reshape(512, NW),
         preferred_element_type=F32,
     )
-    final = (both[0:16] + both[16:32]) * (factor * apply_weight) + zs[z].astype(F32)
+    final = (both[0:16] + both[16:32]) * (factor * apply_weight) + zs[(z + NZ - 2 * core) % NZ].astype(F32)
     wait_for(zr, zrr)
     for d in range(3):
         final = final + zr[d].astype(F32)
@@ -417,21 +430,30 @@
         wait_for(rn.at[pl.ds(0, 15)], ns)
         wait_for(rk.at[pl.ds(0, 31)], ks)
 
-    out.wait()
+
+def hand_over(app_in, cn_in, app_out, cn_out, sem):
+    copies = [pltpu.make_async_copy(app_in, app_out, sem.at[4])]
+    for i in range(4):
+        lines = pl.ds(144 * i, 144)
+        copies.append(pltpu.make_async_copy(cn_in.at[lines], cn_out.at[lines], sem.at[i]))
+    for copy in copies:
+        copy.start()
+    for copy in copies:
+        copy.wait()
 
 
 def per_device(inputs, out_grads, proj_in, proj_out, curvature):
     dma = pltpu.SemaphoreType.DMA
     vm = pltpu.VMEM
     hbm = pl.BlockSpec(memory_space=pl.ANY)
-    return pl.pallas_call(
+    applied, curvature_new = pl.pallas_call(
         kernel,
         out_shape=(
-            jax.ShapeDtypeStruct((OWN, NW), F32),
-            jax.ShapeDtypeStruct((KW, NW), BF16),
+            pltpu.VMEM((OWN, NW), F32),
+            pltpu.VMEM((KW, NW), BF16),
         ),
         in_specs=[hbm] * 5,
-        out_specs=(pl.BlockSpec(memory_space=pltpu.VMEM), hbm),
+        out_specs=(pl.BlockSpec(memory_space=pltpu.VMEM),) * 2,
         scratch_shapes=[
             vm(inputs.shape, BF16), vm(out_grads.shape, BF16), vm(proj_in.shape, BF16),
             vm(proj_out.shape, BF16), vm((KP, NW), BF16),
@@ -441,17 +463,31 @@
             vm((PIN, 512), F32), vm((256, 512), BF16), vm((256, 512), BF16),
             vm((16, PIN * POUT), BF16),
             vm((32, 16, NW), BF16), vm((32, 16, KP), BF16), vm((KP, 512), BF16),
-            vm((KW, NW), BF16), vm((32, 16, NW), BF16), vm((2, 4, 4, 16, NW), BF16),
+            vm((32, 16, NW), BF16), vm((2, 4, 4, 16, NW), BF16),
             vm((4, 16, NW), BF16), vm((3, 16, NW), BF16),
             vm((16, 512), BF16), vm((16, 512), BF16), vm((7, 16, 512), BF16), vm((16, 512), BF16),
             dma((5,)), dma, dma, dma, dma, dma, dma, dma, dma, dma, dma, dma, dma, dma, dma,
             dma, dma((4,)), dma, dma((2, 4, 4)), dma, dma, dma, dma((3,)), dma, dma,
-            dma, dma((2, 4, 4)), dma, dma, dma, dma, dma, dma, dma,
+            dma, dma((2, 4, 4)), dma, dma, dma, dma, dma, dma,
         ],
         compiler_params=pltpu.CompilerParams(
-            collective_id=0, has_side_effects=True, vmem_limit_bytes=60 * 2**20
+            collective_id=0, has_side_effects=True, vmem_limit_bytes=48 * 2**20
         ),
-    )(inputs, out_grads, proj_in, proj_out, curvature)
+    )(*(
+        pltpu.with_memory_space_constraint(a, pltpu.HBM)
+        for a in (inputs, out_grads, proj_in, proj_out, curvature)
+    ))
+    return pl.pallas_call(
+        hand_over,
+        out_shape=(
+            jax.ShapeDtypeStruct((OWN, NW), F32),
+            jax.ShapeDtypeStruct((KW, NW), BF16),
+        ),
+        in_specs=[hbm] * 2,
+        out_specs=(hbm, hbm),
+        scratch_shapes=[dma((5,))],
+        compiler_params=pltpu.CompilerParams(vmem_limit_bytes=2 * 2**20),
+    )(applied, curvature_new)
 
 
 def solution(mesh):

time: 84.8 us -> 80.3 us (0.947)
  local copies, waits for them, and re-layouts: 4.01 us -> 0 us
    unnamed x2 -> x0, local copies, waits for them, and re-layouts: 4.01 us -> none
    pallas_call x1 -> x2, Pallas kernels: 79.4 us -> 79 us  [the longest x1 77.9 us: per_device(): pl.pallas_call(kernel, out_shape=(pltpu.VMEM((OWN, NW), F32), pltpu.VMEM(...]
where the time goes in v5:
time: 80.3 us; the launch traced here: 79.7 us
  Pallas kernels  79 us (98%)
    pallas_call x1, Pallas kernels, per_device(): pl.pallas_call(kernel, out_shape=(pltpu.VMEM((OWN, NW), F32), pltpu.VMEM(...  77.9 us

profile of v5, /device:TPU:6, one launch (start us, length us, event | category | flops | bytes accessed | tf_op | source)
XLA Modules:
  0.0 79.7 jit_solution(6610574746808682492)
XLA Ops:
  0.6 77.9 %shard_map.68 = (f32[15,1152]{1,0:T(8,128)S(1)}, bf16[576,1152]{1,0:T(8,128)(2,1)S(1)}) custom-call(bf16[960,896]{1,0:T(8,128)(2,1)} %x_hbm.1, bf16[960,256]{1,0:T(8,128)(2,1)} %g_hbm.1, bf16[96,896]{1,0:T(8,128)(2,1)} %wi_hbm.1, bf16[192,256]{1,0:T(8,128)(2,1)} %wo_hbm.1, bf16[576,1152]{1,0:T(8,128)(2,1)} %c_hbm.1), custom_call_target="tpu_custom_call" | custom-call | tf_op jit(solution)/shard_map/pallas_call | solution.py:449
  78.5 1.1 %shard_map.69 = (f32[15,1152]{1,0:T(8,128)}, bf16[576,1152]{1,0:T(8,128)(2,1)}) custom-call(f32[15,1152]{1,0:T(8,128)S(1)} %get-tuple-element.4.app_in, bf16[576,1152]{1,0:T(8,128)(2,1)S(1)} %get-tuple-element.5.cn_in), custom_call_target="tpu_custom_call" | custom-call | tf_op jit(solution)/shard_map/pallas_call | solution.py:480

commit v6 on v5

--- a/solution.py
+++ b/solution.py
@@ -12,7 +12,7 @@
 PIN = 96
 POUT = 192
 FEATS = PIN + POUT
-ZR = 96
+ZR = 112
 YR = FEATS - ZR
 SEQ = 32
 EXAMPLES = 480
@@ -219,7 +219,32 @@
             == lax.broadcasted_iota(jnp.int32, (16, 512), 0)
         )
 
-        def form(i, carry):
+        def n_slice(cc):
+            return rows.at[:, pl.ds(pl.multiple_of(cc * NW, 128), NW)]
+
+        def k_slice(kk):
+            return rows.at[:, pl.ds(pl.multiple_of((kk // 2) * NW + (kk % 2) * 512, 128), KP)]
+
+        def to_col(cc):
+            @pl.when(cc != c)
+            def _():
+                send(n_slice(cc), rn.at[own_slot], ns, nr, col_dev(cc))
+
+            @pl.when(cc == c)
+            def _():
+                pltpu.make_async_copy(n_slice(cc), rn.at[own_slot], nr).start()
+
+        def to_hid(kk):
+            @pl.when(kk != h)
+            def _():
+                send(k_slice(kk), rk.at[own_slot], ks, kr, (kk, c))
+
+            @pl.when(kk == h)
+            def _():
+                pltpu.make_async_copy(k_slice(kk), rk.at[own_slot], kr).start()
+
+        def form(step, carry):
+            i = (x + 3 - step) % 4
             def spread(odd):
                 return jnp.concatenate(
                     [
@@ -243,38 +268,15 @@
                 )
                 at = pl.multiple_of(i * 4608 + 384 * q, 128)
                 rows[:, pl.ds(at, 384)] = three.astype(BF16)
+            for dc in range(2):
+                to_col(4 * i + 2 * (1 - zh) + dc)
+            for dk in range(8):
+                to_hid(8 * i + dk)
+            for dc in range(2):
+                to_col(4 * i + 2 * zh + dc)
             return carry
 
         lax.fori_loop(0, 4, form, 0)
-
-        def n_slice(cc):
-            return rows.at[:, pl.ds(pl.multiple_of(cc * NW, 128), NW)]
-
-        def k_slice(kk):
-            return rows.at[:, pl.ds(pl.multiple_of((kk // 2) * NW + (kk % 2) * 512, 128), KP)]
-
-        pltpu.make_async_copy(n_slice(c), rn.at[own_slot], nr).start()
-        pltpu.make_async_copy(k_slice(h), rk.at[own_slot], kr).start()
-
-        def to_col(dx, dz, dc):
-            cc = (((x + dx) % 4) * 2 + (zh + dz) % 2) * 2 + (core + dc) % 2
-            send(n_slice(cc), rn.at[own_slot], ns, nr, col_dev(cc))
-
-        def to_hid(dy, dz):
-            kk = ((y + dy) % NY) * NZ + (z + dz) % NZ
-            send(k_slice(kk), rk.at[own_slot], ks, kr, (kk, c))
-
-        for dx in (2, 1, 3, 0):
-            for dc in range(2):
-                to_col(dx, 1, dc)
-        for dy in (4, 3, 5, 2, 6, 1, 7, 0):
-            for dz in range(NZ):
-                if dy + dz > 0:
-                    to_hid(dy, dz)
-        for dx in (2, 1, 3, 0):
-            for dc in range(2):
-                if dx + dc > 0:
-                    to_col(dx, 0, dc)
 
     up, down = (y + 1) % NY, (y + NY - 1) % NY
 

time: 80.3 us -> 78.8 us (0.981)
  Pallas kernels: 79 us -> 77.3 us
    pallas_call x1, Pallas kernels: 77.9 us -> 76.2 us  [per_device(): pl.pallas_call(kernel, out_shape=(pltpu.VMEM((OWN, NW), F32), pltpu.VMEM(...]
where the time goes in v6:
time: 78.8 us; the launch traced here: 77.9 us
  Pallas kernels  77.3 us (98%)
    pallas_call x1, Pallas kernels, per_device(): pl.pallas_call(kernel, out_shape=(pltpu.VMEM((OWN, NW), F32), pltpu.VMEM(...  76.2 us

profile of v6, /device:TPU:6, one launch (start us, length us, event | category | flops | bytes accessed | tf_op | source)
XLA Modules:
  0.0 77.9 jit_solution(8847916757654053758)
XLA Ops:
  0.6 76.2 %shard_map.68 = (f32[15,1152]{1,0:T(8,128)S(1)}, bf16[576,1152]{1,0:T(8,128)(2,1)S(1)}) custom-call(bf16[960,896]{1,0:T(8,128)(2,1)} %x_hbm.1, bf16[960,256]{1,0:T(8,128)(2,1)} %g_hbm.1, bf16[96,896]{1,0:T(8,128)(2,1)} %wi_hbm.1, bf16[192,256]{1,0:T(8,128)(2,1)} %wo_hbm.1, bf16[576,1152]{1,0:T(8,128)(2,1)} %c_hbm.1), custom_call_target="tpu_custom_call" | custom-call | tf_op jit(solution)/shard_map/pallas_call | solution.py:451
  76.8 1.1 %shard_map.69 = (f32[15,1152]{1,0:T(8,128)}, bf16[576,1152]{1,0:T(8,128)(2,1)}) custom-call(f32[15,1152]{1,0:T(8,128)S(1)} %get-tuple-element.4.app_in, bf16[576,1152]{1,0:T(8,128)(2,1)S(1)} %get-tuple-element.5.cn_in), custom_call_target="tpu_custom_call" | custom-call | tf_op jit(solution)/shard_map/pallas_call | solution.py:482

commit v7 on v6

--- a/solution.py
+++ b/solution.py
@@ -47,7 +47,7 @@
     part, q1, qs, q2, r1, s1, r2, s2, r3, featv, ge, go, rows,
     rn, rk, rkt, p, rp, zs, zr, sp, sq, sr, sall,
     in_sem, q1s, q1r, q2s, q2r, a1s, a1r, a2s, a2r, a3s, a3r, ns, nr, ks, kr,
-    zas, zar, yas, yar, khs, khr, kxs, kxr, kcs, kcr,
+    zas, zar, yas, yar, khs, khr, kxs, kyr, kxr, kcs, kcr,
     rps, rpr, zrs, zrr, scs, scr, sms, smr,
 ):
     h = lax.axis_index("hid")
@@ -299,6 +299,13 @@
     wait_for(rk.at[pl.ds(k_base, 2)], kr)
     k_two = rk.at[pl.ds(k_base, 2)]
     send(k_two, k_two, khs, khr, col_dev(zh_c))
+
+    def k_over_x(two, rsem):
+        for d in range(1, 4):
+            to = (((x + d) % 4) * 2 + zh) * 2 + core
+            send(two, two, kxs, rsem.at[d - 1], col_dev(to))
+
+    k_over_x(k_two, kyr)
     for j in range(1, NZ):
         wait_for(rn.at[block_slot(y, (z + j) % NZ)], zar.at[j])
         for way in range(2):
@@ -333,14 +340,14 @@
                 send(src, rp.at[way, step, j], rps, rpr.at[way, step, j],
                      hid_dev(up if way == 0 else down, z))
 
-    wait_for(rk.at[pl.ds(core * 16 + x * 4 + (1 - zh) * 2, 2)], khr)
-    k_four = rk.at[pl.ds(core * 16 + x * 4, 4)]
-    for d in range(1, 4):
-        xx = (x + d) % 4
-        send(k_four, k_four, kxs, kxr.at[d - 1], col_dev((xx * 2 + zh) * 2 + core))
+    k_other = rk.at[pl.ds(core * 16 + x * 4 + (1 - zh) * 2, 2)]
+    wait_for(k_other, khr)
+    k_over_x(k_other, kxr)
     y_round(1)
     for d in range(1, 4):
-        wait_for(rk.at[pl.ds(core * 16 + ((x + 4 - d) % 4) * 4, 4)], kxr.at[d - 1])
+        at = core * 16 + ((x + 4 - d) % 4) * 4
+        wait_for(rk.at[pl.ds(at + zh * 2, 2)], kyr.at[d - 1])
+        wait_for(rk.at[pl.ds(at + (1 - zh) * 2, 2)], kxr.at[d - 1])
     k_all = rk.at[pl.ds(core * 16, 16)]
     send(k_all, k_all, kcs, kcr, col_dev(m * 2 + 1 - core))
     y_round(2)
@@ -469,7 +476,7 @@
             vm((4, 16, NW), BF16), vm((3, 16, NW), BF16),
             vm((16, 512), BF16), vm((16, 512), BF16), vm((7, 16, 512), BF16), vm((16, 512), BF16),
             dma((5,)), dma, dma, dma, dma, dma, dma, dma, dma, dma, dma, dma, dma, dma, dma,
-            dma, dma((4,)), dma, dma((2, 4, 4)), dma, dma, dma, dma((3,)), dma, dma,
+            dma, dma((4,)), dma, dma((2, 4, 4)), dma, dma, dma, dma((3,)), dma((3,)), dma, dma,
             dma, dma((2, 4, 4)), dma, dma, dma, dma, dma, dma,
         ],
         compiler_params=pltpu.CompilerParams(

time: 78.8 us -> 79 us (level)
  no operation moved by 1% of the time
where the time goes in v7:
time: 79 us; the launch traced here: 77.9 us
  Pallas kernels  77.3 us (98%)
    pallas_call x1, Pallas kernels, per_device(): pl.pallas_call(kernel, out_shape=(pltpu.VMEM((OWN, NW), F32), pltpu.VMEM(...  76.2 us

profile of v7, /device:TPU:6, one launch (start us, length us, event | category | flops | bytes accessed | tf_op | source)
XLA Modules:
  0.0 77.9 jit_solution(3028540670075400278)
XLA Ops:
  0.6 76.2 %shard_map.68 = (f32[15,1152]{1,0:T(8,128)S(1)}, bf16[576,1152]{1,0:T(8,128)(2,1)S(1)}) custom-call(bf16[960,896]{1,0:T(8,128)(2,1)} %x_hbm.1, bf16[960,256]{1,0:T(8,128)(2,1)} %g_hbm.1, bf16[96,896]{1,0:T(8,128)(2,1)} %wi_hbm.1, bf16[192,256]{1,0:T(8,128)(2,1)} %wo_hbm.1, bf16[576,1152]{1,0:T(8,128)(2,1)} %c_hbm.1), custom_call_target="tpu_custom_call" | custom-call | tf_op jit(solution)/shard_map/pallas_call | solution.py:458
  76.8 1.1 %shard_map.69 = (f32[15,1152]{1,0:T(8,128)}, bf16[576,1152]{1,0:T(8,128)(2,1)}) custom-call(f32[15,1152]{1,0:T(8,128)S(1)} %get-tuple-element.4.app_in, bf16[576,1152]{1,0:T(8,128)(2,1)S(1)} %get-tuple-element.5.cn_in), custom_call_target="tpu_custom_call" | custom-call | tf_op jit(solution)/shard_map/pallas_call | solution.py:489
